TPU v7x, 512 devices: a whole 4x4x16 slice. The times are simulated.
512 devices in a mesh: dp: 64 (over x, z), mp: 8 (over y, core).
Axes of the slice: x: 4, y: 4, z: 16, core: 2. Of those that a mesh axis runs over, the one named last changes fastest.
Arguments:
- query: bfloat16 [32768, 2048], P('dp', 'mp'), may hold values from -2.5 to 2.5
- key: bfloat16 [32768, 2048], P('dp', 'mp'), may hold values from -2.5 to 2.5
- value: bfloat16 [32768, 2048], P('dp', 'mp'), may hold values from -6 to 6
- cotangent: bfloat16 [32768, 4096], P('dp', 'mp'), may hold values from -16 to 16
- weight_out: bfloat16 [4096, 2048], P('dp', 'mp'), may hold values from -0.125 to 0.125
- keep_attn: int32 [32, 64], P('mp', 'dp'), may hold values from 0 to 65279
- keep_out: int32 [64, 4096], P('dp', 'mp'), may hold values from 0 to 65279
- doc_lengths: int32 [64, 8], P('dp'), may hold values from 1 to 256, 512 in all within a row
Outputs:
- grad_query: bfloat16 [32768, 2048], P('dp', 'mp')
- grad_key: bfloat16 [32768, 2048], P('dp', 'mp')
- grad_value: bfloat16 [32768, 2048], P('dp', 'mp')
- grad_weight: float32 [4096, 2048], P('dp', 'mp')
All inputs are finite; a program needn't handle non-finite values.
Results may differ from a plain program's by a relative error of at most 0.02.
Values may be sent and summed in bfloat16 or wider, within the bound.
A program may use at most 64 MiB of HBM per device.

v0:
```python
import jax
import jax.numpy as jnp
from jax import lax
from jax.sharding import PartitionSpec as P

DK = 64
SEQ = 512


DROP_SCALE = 1.0 / 0.9


def mix_bits(stream, first, second):
    x = (
        stream * jnp.int32(-1640531535)
        + first * jnp.int32(668265263)
        + second * jnp.int32(374761393)
    )
    x = x ^ lax.shift_right_logical(x, jnp.int32(16))
    x = x * jnp.int32(73244475)
    x = x ^ lax.shift_right_logical(x, jnp.int32(15))
    x = x * jnp.int32(-2048144789)
    x = x ^ lax.shift_right_logical(x, jnp.int32(16))
    return ((x & jnp.int32(65535)) % jnp.int32(10) < jnp.int32(9)).astype(jnp.float32)


def segment_ids(lengths):
    ends = jnp.cumsum(lengths)
    places = jnp.arange(SEQ, dtype=jnp.int32)
    return jnp.sum((ends[None, :] <= places[:, None]).astype(jnp.int32), axis=1)


def probs_row(qrow, krow, streams, lengths):
    seg = segment_ids(lengths)
    same = seg[:, None] == seg[None, :]
    places = jnp.arange(SEQ, dtype=jnp.int32)
    keep = mix_bits(streams[:, None, None], places[None, :, None], places[None, None, :])
    scores = jnp.einsum("qhd,khd->hqk", qrow, krow, preferred_element_type=jnp.float32)
    scores = jnp.where(same[None], scores, -1e30)
    probs = jax.nn.softmax(scores, axis=-1)
    kept = (probs * keep * DROP_SCALE).astype(jnp.bfloat16)
    return (probs, keep, kept)


def grads_row(qrow, krow, vrow, grow, probs, keep, kept):
    grad_value = jnp.einsum("hqk,qhd->khd", kept, grow, preferred_element_type=jnp.float32).astype(
        jnp.bfloat16
    )
    grad_probs = (
        jnp.einsum("qhd,khd->hqk", grow, vrow, preferred_element_type=jnp.float32)
        * keep
        * DROP_SCALE
    )
    delta = jnp.sum(probs * grad_probs, axis=-1, keepdims=True)
    grad_scores = (probs * (grad_probs - delta)).astype(jnp.bfloat16)
    grad_query = jnp.einsum(
        "hqk,khd->qhd", grad_scores, krow, preferred_element_type=jnp.float32
    ).astype(jnp.bfloat16)
    grad_key = jnp.einsum(
        "hqk,qhd->khd", grad_scores, qrow, preferred_element_type=jnp.float32
    ).astype(jnp.bfloat16)
    return (grad_query, grad_key, grad_value)


def full_row(args):
    qrow, krow, vrow, grow, streams, lengths = args
    probs, keep, kept = probs_row(qrow, krow, streams, lengths)
    context = jnp.einsum("hqk,khd->qhd", kept, vrow, preferred_element_type=jnp.float32).astype(
        jnp.bfloat16
    )
    grad_query, grad_key, grad_value = grads_row(qrow, krow, vrow, grow, probs, keep, kept)
    return (context, grad_query, grad_key, grad_value)


def shards(query, key, value, cotangent, weight_out, keep_attn, keep_out, doc_lengths):
    rows_here = doc_lengths.shape[0]
    tok_here = query.shape[0]
    inner_here = query.shape[1]
    heads_here = inner_here // DK
    feats_here = cotangent.shape[1]
    places = jnp.arange(SEQ, dtype=jnp.int32)
    keep_o = mix_bits(keep_out[:, None, :], places[None, :, None], jnp.int32(0)).reshape(
        tok_here, feats_here
    )
    dropped_part = (cotangent.astype(jnp.float32) * keep_o * DROP_SCALE).astype(jnp.bfloat16)
    dropped = lax.all_gather(dropped_part, "mp", axis=1, tiled=True)

    def split_rows(x):
        return x.reshape(rows_here, SEQ, heads_here, DK)

    streams = jnp.transpose(keep_attn, (1, 0))
    q_rows = split_rows(query)
    k_rows = split_rows(key)
    v_rows = split_rows(value)
    columns = dropped
    total = jnp.dot(
        columns,
        lax.all_gather(weight_out, "dp", axis=0, tiled=True),
        preferred_element_type=jnp.float32,
    )
    grad_context = total.astype(jnp.bfloat16)
    context, grad_query, grad_key, grad_value = lax.map(
        full_row, (q_rows, k_rows, v_rows, split_rows(grad_context), streams, doc_lengths)
    )
    weight_context = context.reshape(tok_here, inner_here)
    columns = dropped
    grad_weight = lax.psum_scatter(
        lax.dot_general(
            columns, weight_context, (((0,), (0,)), ((), ())), preferred_element_type=jnp.float32
        ),
        "dp",
        scatter_dimension=0,
        tiled=True,
    )
    return (
        grad_query.reshape(tok_here, inner_here),
        grad_key.reshape(tok_here, inner_here),
        grad_value.reshape(tok_here, inner_here),
        grad_weight,
    )


def solution(mesh):
    in_specs = (
        P("dp", "mp"),
        P("dp", "mp"),
        P("dp", "mp"),
        P("dp", "mp"),
        P("dp", "mp"),
        P("mp", "dp"),
        P("dp", "mp"),
        P("dp", None),
    )
    out_specs = (P("dp", "mp"), P("dp", "mp"), P("dp", "mp"), P("dp", "mp"))
    return jax.shard_map(shards, mesh=mesh, in_specs=in_specs, out_specs=out_specs, check_vma=False)
```

profile of v0, /device:TPU:16, one launch (start us, length us, event | category | flops | bytes accessed | tf_op | source)
XLA Modules:
  0.0 906.4 jit_solution(7318463990381123030)
XLA Ops:
  7.2 0.0 all-gather.3.cloned.1.call-start
  7.2 0.7 broadcast_multiply_fusion
  7.9 3.0 multiply_convert_fusion.2
  10.9 0.0 all-gather.3.cloned.1.call-update
  10.9 0.0 all-gather.5.cloned.1.call-start
  10.9 0.7 all-gather.5.cloned.1.call-update
  11.6 0.0 reduce-scatter.2.cloned.1.call-start
  11.7 1.1 copy.35
  12.8 1.1 copy.36
  13.9 1.1 copy.37
  15.0 0.8 reduce-window.8
  15.8 0.1 convert_reduce_fusion
  15.9 0.7 multiply_bitcast_fusion
  16.6 0.1 broadcast_add_fusion
  16.6 0.2 broadcast_compare_fusion
  16.9 3.6 fusion.19
  20.5 6.2 convolution_convert_fusion
  26.7 27.1 %all-gather.3.cloned.1.call-done = bf16[512,4096]{1,0:T(8,128)(2,1)} async-done(((bf16[512,512]{1,0:T(8,128)(2,1)}), bf16[512,4096]{1,0:T(8,128)(2,1)}) %all-gather.3.cloned.1.call-update) | async-done | bytes 4194320 | tf_op jit(solution)/shard_map/all_gather | solution.py:86
  53.8 5.5 fusion.20
  59.3 0.0 reduce-scatter.2.cloned.1.call-update
  59.3 139.7 %all-gather.5.cloned.1.call-done = bf16[4096,256]{1,0:T(8,128)(2,1)} async-done(((bf16[64,256]{1,0:T(8,128)(2,1)}), bf16[4096,256]{1,0:T(8,128)(2,1)}) %all-gather.5.cloned.1.call-update) | async-done | bytes 2097168 | tf_op jit(solution)/shard_map/all_gather | solution.py:98
  199.1 0.0 copy-start
  199.1 4.3 convolution_convert_fusion.4
  203.4 0.0 copy-done
  203.4 4.5 convolution_convert_fusion.2
  207.8 0.8 copy.44
  208.7 0.0 copy-start.1
  208.7 6.5 multiply_reduce_fusion
  215.2 0.0 copy-done.1
  215.2 4.6 multiply_convert_fusion.1
  219.8 0.5 convolution_convert_fusion.1
  220.3 0.8 copy.42
  221.2 0.7 convolution_convert_fusion.3
  221.9 0.8 copy.43
  222.7 677.2 %reduce-scatter.2.cloned.1.call-done = f32[64,256]{1,0:T(8,128)} async-done(((f32[4096,256]{1,0:T(8,128)}), f32[64,256]{1,0:T(8,128)}) %reduce-scatter.2.cloned.1.call-update) | async-done | bytes 65552 | tf_op jit(solution)/shard_map/reduce_scatter | solution.py:107
  (2 shorter events, 0.0 us)
Async XLA Ops:
  7.2 46.7 %all-gather.3.cloned.1.call-start = ((), (), s32[]{:S(2)}) async-start(), calls=%async_computation.1 | async-start | bytes 4718592 | tf_op jit(solution)/shard_map/all_gather | solution.py:86
  10.9 188.2 %all-gather.5.cloned.1.call-start = ((), (), s32[]{:S(2)}) async-start(), calls=%async_computation.2 | async-start | bytes 2129920 | tf_op jit(solution)/shard_map/all_gather | solution.py:98
  11.6 888.3 %reduce-scatter.2.cloned.1.call-start = ((), (), s32[]{:S(2)}) async-start(), calls=%async_computation.3 | async-start | bytes 4259840 | tf_op jit(solution)/shard_map/reduce_scatter | solution.py:107
  199.1 4.3 copy-start
  208.7 6.5 copy-start.1
Sparse Core Ops, SparseCore 0:
  11.0 42.7 all-gather.2
  56.8 142.2 all-gather.4
  204.0 695.8 reduce-scatter.1
where the time goes:
time: 907 us; the launch traced here: 906 us
  waiting for transfers between devices  845 us (93%)
  matrix products  31.7 us (3%)
  between operations  13.8 us (2%)
  other arithmetic  10.1 us (1%)
    reduce_scatter x1, waiting for transfers between devices, shards(): lax.psum_scatter(lax.dot_general(columns, weight_context, (((0,), (0,)),...  677 us
    all_gather x1, waiting for transfers between devices, shards(): lax.all_gather(weight_out, 'dp', axis=0, tiled=True)  140 us
    all_gather x1, waiting for transfers between devices, shards(): dropped = lax.all_gather(dropped_part, 'mp', axis=1, tiled=True)  27.1 us
  transfers between devices with their start and end apart: 3, of which 3 were waited for; matrix products, arithmetic and copies ran while one was open for 5% of the time, Pallas kernels for 0%

commit v1 on v0

v1 whole, which is shorter than its diff:
```python
import jax
import jax.numpy as jnp
from jax import lax
from jax.experimental import pallas as pl
from jax.experimental.pallas import tpu as pltpu
from jax.sharding import PartitionSpec as P

MESH = pl.DeviceIdType.MESH
BF = jnp.bfloat16
F32 = jnp.float32
I32 = jnp.int32
DK = 64
SEQ = 512
HEADS = 4
FEAT = 256
NX, NY, NZ, NEAR = 4, 4, 16, 4
DROP = 0.9
DROP_SCALE = 1.0 / 0.9
TENTH = 429496730
TURN = -1717986918 + 1000
NINE = -(1 << 31) + 200000000


def kept_bits(x):
    x = x ^ lax.shift_right_logical(x, jnp.int32(16))
    x = x * jnp.int32(73244475)
    x = x ^ lax.shift_right_logical(x, jnp.int32(15))
    x = x * jnp.int32(-2048144789)
    x = x ^ lax.shift_right_logical(x, jnp.int32(16))
    return (x & jnp.int32(65535)) * jnp.int32(TENTH) + jnp.int32(TURN) >= jnp.int32(NINE)


def kernel(
    q_ref, k_ref, v_ref, cot_ref, w_ref, ka_ref, ko_ref, dl_ref,
    gq_ref, gk_ref, gv_ref, gw_ref,
    drt, wx, wt, qt_s, kt_s, vt_s, gt_s, g_s, ctxf, ctx, seg_s, spot_s, s_s, sp_s, kp_s, gs_s, gqt_s, gka, gva,
    hop_s, hop_r, fin_s, fin_r, own, near_s, near_r, far_s, far_r,
    ysend, yrecv, wxsend, wxrecv, wsend, wrecv, xsend, xrecv, nsend, nrecv, fsend, frecv,
):
    dp, mp = lax.axis_index("dp"), lax.axis_index("mp")
    x, z = dp // NZ, lax.rem(dp, NZ)
    y, c = mp // 2, lax.rem(mp, 2)
    near, far = lax.rem(z, NEAR), z // NEAR

    def at(dx=0, dy=0, dz=0, dc=0):
        px, py = lax.rem(x + dx + NX, NX), lax.rem(y + dy + NY, NY)
        pz, pc = lax.rem(z + dz + NZ, NZ), lax.rem(c + dc, 2)
        return (px * NZ + pz, py * 2 + pc)

    def near_peer(j):
        return (x * NZ + far * NEAR + lax.rem(near + j, NEAR), mp)

    core, yp, ym = at(dc=1), at(dy=1), at(dy=-1)
    xp, xm, x2, zp, zm = at(dx=1), at(dx=-1), at(dx=2), at(dz=1), at(dz=-1)
    near_peers = [near_peer(j) for j in range(1, NEAR)]
    far_peers = [at(dz=NEAR * j) for j in range(1, NEAR)]
    greeted = [core, yp, ym, xp, xm, x2, zp, zm] + near_peers + far_peers
    barrier = pltpu.get_barrier_semaphore()
    for peer in greeted:
        pl.semaphore_signal(barrier, inc=1, device_id=peer, device_id_type=MESH)

    pending = []

    def send(src, dst, ssem, rsem, peer):
        copy = pltpu.make_async_remote_copy(
            src_ref=src, dst_ref=dst, send_sem=ssem, recv_sem=rsem, device_id=peer, device_id_type=MESH
        )
        copy.start()
        pending.append(copy)

    def arrived(ref, ssem, rsem):
        pltpu.make_async_remote_copy(
            src_ref=ref, dst_ref=ref, send_sem=ssem, recv_sem=rsem, device_id=core, device_id_type=MESH
        ).wait_recv()

    spots = lax.broadcasted_iota(I32, (SEQ, 128), 0)
    first = spots * jnp.int32(668265263)
    for j in range(4):
        lanes = pl.ds(j * 128, 128)
        word = first + ko_ref[:, lanes] * jnp.int32(-1640531535)
        part = jnp.where(kept_bits(word), cot_ref[:, lanes].astype(F32) * DROP_SCALE, 0.0).astype(BF)
        drt[mp, j // 2, pl.ds((j % 2) * 128, 128), :] = part.T
    wx[x] = w_ref[...]

    pl.semaphore_wait(barrier, len(greeted))

    for i, peer in enumerate((xp, xm, x2)):
        send(wx.at[x], wx.at[x], wxsend.at[i], wxrecv.at[x], peer)
    ysends = [0]

    def ysend_to(block, piece, peer):
        ref = drt.at[block, piece]
        send(ref, ref, ysend.at[ysends[0]], yrecv.at[block, piece], peer)
        ysends[0] += 1

    for piece in range(2):
        for peer in (yp, ym, core):
            ysend_to(mp, piece, peer)

    def yblock(dy, dc=0):
        return lax.rem(y + dy + NY, NY) * 2 + lax.rem(c + dc, 2)

    def ywait(block, piece):
        arrived(drt.at[block, piece], ysend.at[0], yrecv.at[block, piece])

    def y_step(dy, piece):
        block = yblock(dy)
        ywait(block, piece)
        if dy == -1 and piece == 0:
            ysend_to(block, piece, yp)
        if dy == 1 and piece == 1:
            ysend_to(block, piece, ym)
        ysend_to(block, piece, core)

    wsends = [0]

    def ring_send(block, sub, peer):
        ref = wt.at[block, sub]
        send(ref, ref, wsend.at[wsends[0]], wrecv.at[block, sub], peer)
        wsends[0] += 1

    def ring_start():
        for j in (1, 2, 3):
            block = lax.rem(x + j, NX)
            arrived(wx.at[block], wxsend.at[0], wxrecv.at[block])
        own_w = jnp.concatenate([wx[j] for j in range(NX)], axis=0).T
        for sub in range(2):
            wt[z, sub] = own_w[sub * 128:(sub + 1) * 128]
            ring_send(z, sub, zp)
            ring_send(z, sub, zm)

    def ring_step(k):
        for sub in range(2):
            block = lax.rem(z - k + NZ, NZ)
            arrived(wt.at[block, sub], wsend.at[0], wrecv.at[block, sub])
            if k < NZ // 2:
                ring_send(block, sub, zp)
            if k < NZ // 2:
                block = lax.rem(z + k, NZ)
                arrived(wt.at[block, sub], wsend.at[0], wrecv.at[block, sub])
                if k < NZ // 2 - 1:
                    ring_send(block, sub, zm)

    ends, total = [], 0
    for j in range(8):
        total = total + dl_ref[0, j]
        ends.append(total)

    def segments(places):
        seg = jnp.zeros(places.shape, I32)
        for end in ends:
            seg = seg + (places >= end).astype(I32)
        return seg

    seg_s[...] = segments(spots)
    spot_s[...] = spots * jnp.int32(374761393)
    qt_s[...] = q_ref[...].T
    kt_s[...] = k_ref[...].T
    vt_s[...] = v_ref[...].T
    head_rows = lax.broadcasted_iota(I32, (FEAT, SEQ), 0) // DK
    head_lanes = lax.broadcasted_iota(I32, (SEQ, FEAT), 1) // DK
    ROWS = 64

    def forward(h):
        mine = jnp.where(head_rows == h, qt_s[...].astype(F32), 0.0).astype(BF)
        s_s[...] = jnp.dot(k_ref[...], mine, preferred_element_type=F32)

        def tile(t, carry):
            lanes = pl.ds(pl.multiple_of(t * 128, 128), 128)
            here = lax.broadcasted_iota(I32, (1, 128), 1) + t * 128
            seg_here = segments(here)
            word_here = here * jnp.int32(668265263) + ka_ref[h, 0] * jnp.int32(-1640531535)
            top = jnp.full((ROWS, 128), -1e30, F32)
            for r in range(0, SEQ, ROWS):
                rows = pl.ds(r, ROWS)
                got = jnp.where(seg_s[rows, :] == seg_here, s_s[rows, lanes], -1e30)
                s_s[rows, lanes] = got
                top = jnp.maximum(top, got)
            top = jnp.max(top, axis=0, keepdims=True)
            mass = jnp.zeros((ROWS, 128), F32)
            for r in range(0, SEQ, ROWS):
                rows = pl.ds(r, ROWS)
                got = jnp.exp(s_s[rows, lanes] - top)
                s_s[rows, lanes] = got
                mass = mass + got
            scale = DROP_SCALE / jnp.sum(mass, axis=0, keepdims=True)
            for r in range(0, SEQ, ROWS):
                rows = pl.ds(r, ROWS)
                keep = kept_bits(spot_s[rows, :] + word_here)
                got = s_s[rows, lanes] * scale
                sp_s[h, rows, lanes] = jnp.where(keep, got, -got)
                kp_s[h, rows, lanes] = jnp.where(keep, got, 0.0).astype(BF)
            return carry

        lax.fori_loop(0, 4, tile, 0)
        ctxf[pl.ds(h * DK, DK), :] = jnp.dot(vt_s[pl.ds(h * DK, DK), :], kp_s[h], preferred_element_type=F32)

    def backward(h):
        mine = jnp.where(head_rows == h, gt_s[...].astype(F32), 0.0).astype(BF)
        s_s[...] = jnp.dot(v_ref[...], mine, preferred_element_type=F32)
        rows_h = pl.ds(h * DK, DK)
        delta = DROP * jnp.sum(gt_s[rows_h, :].astype(F32) * ctxf[rows_h, :], axis=0, keepdims=True)
        for t in range(4):
            lanes = pl.ds(t * 128, 128)
            for r in range(0, SEQ, ROWS):
                rows = pl.ds(r, ROWS)
                d = jnp.broadcast_to(delta[:, t * 128:(t + 1) * 128], (ROWS, 128))
                got = sp_s[h, rows, lanes]
                gs_s[rows, lanes] = (got * jnp.where(got > 0.0, s_s[rows, lanes] - d, d)).astype(BF)
        gqt_s[rows_h, :] = jnp.dot(kt_s[rows_h, :], gs_s[...], preferred_element_type=F32).astype(BF)
        q_h = jnp.where(head_lanes == h, q_ref[...].astype(F32), 0.0).astype(BF)
        g_h = jnp.where(head_lanes == h, g_s[...].astype(F32), 0.0).astype(BF)
        gk = jnp.dot(gs_s[...], q_h, preferred_element_type=F32)
        gv = jnp.dot(kp_s[h], g_h, preferred_element_type=F32)
        if h == 0:
            gka[...] = gk
            gva[...] = gv
        else:
            gka[...] += gk
            gva[...] += gv

    forward(0)
    ring_start()
    forward(1)
    ring_step(1)
    forward(2)
    y_step(1, 0)
    y_step(-1, 0)
    ring_step(2)
    forward(3)
    ctx[...] = ctxf[...].astype(BF).T
    y_step(1, 1)
    y_step(-1, 1)
    ring_step(3)
    y_step(2, 0)
    y_step(2, 1)
    for dy in range(4):
        for piece in range(2):
            ywait(yblock(dy, 1), piece)

    def share(dx, half):
        block = lax.rem(x + dx + NX, NX) * 2 + half
        return jnp.concatenate(
            [jnp.dot(drt[block, piece], ctx[...], preferred_element_type=F32) for piece in range(2)], axis=0
        )

    hop_s[0] = share(2, 0).astype(BF)
    send(hop_s.at[0], hop_r.at[0], xsend.at[0], xrecv.at[0], xp)
    hop_s[1] = share(2, 1).astype(BF)
    send(hop_s.at[1], hop_r.at[1], xsend.at[1], xrecv.at[1], xm)
    fin_s[0] = share(1, 1).astype(BF)
    send(fin_s.at[0], fin_r.at[0], xsend.at[2], xrecv.at[2], xp)
    fin_s[1] = share(-1, 0).astype(BF)
    send(fin_s.at[1], fin_r.at[1], xsend.at[3], xrecv.at[3], xm)
    own[0] = share(0, 0)
    own[1] = share(0, 1)
    ring_step(4)
    fin_s[2] = share(1, 0).astype(BF)
    fin_s[3] = share(-1, 1).astype(BF)
    arrived(hop_r.at[0], xsend.at[0], xrecv.at[0])
    fin_s[2] = (fin_s[2].astype(F32) + hop_r[0].astype(F32)).astype(BF)
    send(fin_s.at[2], fin_r.at[2], xsend.at[4], xrecv.at[4], xp)
    arrived(hop_r.at[1], xsend.at[1], xrecv.at[1])
    fin_s[3] = (fin_s[3].astype(F32) + hop_r[1].astype(F32)).astype(BF)
    send(fin_s.at[3], fin_r.at[3], xsend.at[5], xrecv.at[5], xm)
    ring_step(5)
    ring_step(6)
    ring_step(7)

    for i in range(4):
        arrived(fin_r.at[i], xsend.at[0], xrecv.at[2 + i])
    lower = own[0] + fin_r[1].astype(F32) + fin_r[2].astype(F32)
    upper = own[1] + fin_r[0].astype(F32) + fin_r[3].astype(F32)
    for group in range(4):
        for member in range(4):
            source, row = (lower, group) if group < 2 else (upper, group - 2)
            row = (row * 4 + member) * DK
            near_s[member, group] = source[row:row + DK].astype(BF)
    for i, j in enumerate((1, 2, 3)):
        send(near_s.at[lax.rem(near + j, NEAR)], near_r.at[near], nsend.at[i], nrecv.at[near], near_peers[i])
    ring_step(8)

    def context_part(block):
        half, piece, row = block // 8, (block // 4) % 2, (block % 4) * DK
        left = jnp.concatenate([wt[block, sub] for sub in range(2)], axis=0)
        right = jnp.concatenate([drt[2 * j + half, piece, pl.ds(row, DK), :] for j in range(NX)], axis=0)
        return jnp.dot(left, right, preferred_element_type=F32)

    acc = context_part(0)
    for block in range(1, NZ):
        acc = acc + context_part(block)
    gt_s[...] = acc.astype(BF)
    g_s[...] = gt_s[...].T
    backward(0)
    for j in (1, 2, 3):
        slot = lax.rem(near + j, NEAR)
        arrived(near_r.at[slot], nsend.at[0], nrecv.at[slot])
    total = near_s[near].astype(F32)
    for j in (1, 2, 3):
        total = total + near_r[lax.rem(near + j, NEAR)].astype(F32)
    far_s[...] = total.astype(BF)
    for i, j in enumerate((1, 2, 3)):
        send(far_s.at[lax.rem(far + j, NEAR)], far_r.at[far], fsend.at[i], frecv.at[far], far_peers[i])
    backward(1)
    backward(2)
    backward(3)
    gq_ref[...] = gqt_s[...].T
    gk_ref[...] = gka[...].astype(BF)
    gv_ref[...] = gva[...].astype(BF)
    for j in (1, 2, 3):
        slot = lax.rem(far + j, NEAR)
        arrived(far_r.at[slot], fsend.at[0], frecv.at[slot])
    total = far_s[far].astype(F32)
    for j in (1, 2, 3):
        total = total + far_r[lax.rem(far + j, NEAR)].astype(F32)
    gw_ref[...] = total
    for copy in pending:
        copy.wait_send()


def shards(query, key, value, cotangent, weight_out, keep_attn, keep_out, doc_lengths):
    vmem, smem = pl.BlockSpec(memory_space=pltpu.VMEM), pl.BlockSpec(memory_space=pltpu.SMEM)
    v, dma = pltpu.VMEM, pltpu.SemaphoreType.DMA
    return pl.pallas_call(
        kernel,
        name="attention_backward",
        out_shape=(
            jax.ShapeDtypeStruct((SEQ, FEAT), BF),
            jax.ShapeDtypeStruct((SEQ, FEAT), BF),
            jax.ShapeDtypeStruct((SEQ, FEAT), BF),
            jax.ShapeDtypeStruct((DK, FEAT), F32),
        ),
        in_specs=[vmem, vmem, vmem, vmem, vmem, smem, vmem, smem],
        out_specs=(vmem, vmem, vmem, vmem),
        scratch_shapes=[
            v((8, 2, 256, SEQ), BF),
            v((NX, DK, FEAT), BF),
            v((NZ, 2, 128, FEAT), BF),
            v((FEAT, SEQ), BF),
            v((FEAT, SEQ), BF),
            v((FEAT, SEQ), BF),
            v((FEAT, SEQ), BF),
            v((SEQ, FEAT), BF),
            v((FEAT, SEQ), F32),
            v((SEQ, FEAT), BF),
            v((SEQ, 128), I32),
            v((SEQ, 128), I32),
            v((SEQ, SEQ), F32),
            v((HEADS, SEQ, SEQ), F32),
            v((HEADS, SEQ, SEQ), BF),
            v((SEQ, SEQ), BF),
            v((FEAT, SEQ), BF),
            v((SEQ, FEAT), F32),
            v((SEQ, FEAT), F32),
            v((2, SEQ, FEAT), BF),
            v((2, SEQ, FEAT), BF),
            v((4, SEQ, FEAT), BF),
            v((4, SEQ, FEAT), BF),
            v((2, SEQ, FEAT), F32),
            v((4, 4, DK, FEAT), BF),
            v((4, 4, DK, FEAT), BF),
            v((4, DK, FEAT), BF),
            v((4, DK, FEAT), BF),
            dma((14,)), dma((8, 2)),
            dma((3,)), dma((NX,)),
            dma((32,)), dma((NZ, 2)),
            dma((6,)), dma((6,)),
            dma((3,)), dma((4,)),
            dma((3,)), dma((4,)),
        ],
        compiler_params=pltpu.CompilerParams(
            collective_id=0, has_side_effects=True, vmem_limit_bytes=48 * 2**20
        ),
    )(query, key, value, cotangent, weight_out, keep_attn, keep_out, doc_lengths)


def solution(mesh):
    in_specs = (
        P("dp", "mp"),
        P("dp", "mp"),
        P("dp", "mp"),
        P("dp", "mp"),
        P("dp", "mp"),
        P("mp", "dp"),
        P("dp", "mp"),
        P("dp", None),
    )
    out_specs = (P("dp", "mp"), P("dp", "mp"), P("dp", "mp"), P("dp", "mp"))
    return jax.shard_map(shards, mesh=mesh, in_specs=in_specs, out_specs=out_specs, check_vma=False)
```

time: 907 us -> 89.5 us (0.10)
  the two profiles are of different devices: /device:TPU:16 before, /device:TPU:104 now
where the time goes in v1:
time: 89.5 us; the launch traced here: 89.1 us
  Pallas kernels  80.3 us (90%)
  local copies, waits for them, and re-layouts  8.15 us (9%)
    pallas_call x1, Pallas kernels, shards(): pl.pallas_call(kernel, name='attention_backward', out_shape=(jax.ShapeDty...  80.3 us
    unnamed x19, local copies, waits for them, and re-layouts  8.15 us

profile of v1, /device:TPU:104, one launch (start us, length us, event | category | flops | bytes accessed | tf_op | source)
XLA Modules:
  0.0 89.1 jit_solution(6322017321046548181)
XLA Ops:
  0.6 0.0 copy-start.6
  0.6 0.0 copy-start.5
  0.7 0.8 copy.12.ka_ref
  1.4 0.0 copy-done.6
  1.4 0.0 copy-done.5
  1.4 0.0 copy-start
  1.4 1.0 %copy-done = bf16[512,512]{1,0:T(8,128)(2,1)S(1)} copy-done((bf16[512,512]{1,0:T(8,128)(2,1)S(1)}, bf16[512,512]{1,0:T(8,128)(2,1)}, u32[]{:S(2)}) %copy-start) | copy-done | bytes 524312
  2.5 0.0 copy-start.1
  2.5 0.9 %copy-done.1 = bf16[512,256]{1,0:T(8,128)(2,1)S(1)} copy-done((bf16[512,256]{1,0:T(8,128)(2,1)S(1)}, bf16[512,256]{1,0:T(8,128)(2,1)}, u32[]{:S(2)}) %copy-start.1) | copy-done | bytes 262168
  3.4 0.0 copy-start.2
  3.4 0.9 %copy-done.2 = bf16[512,256]{1,0:T(8,128)(2,1)S(1)} copy-done((bf16[512,256]{1,0:T(8,128)(2,1)S(1)}, bf16[512,256]{1,0:T(8,128)(2,1)}, u32[]{:S(2)}) %copy-start.2) | copy-done | bytes 262168
  4.4 0.0 copy-start.3
  4.4 0.9 %copy-done.3 = bf16[512,256]{1,0:T(8,128)(2,1)S(1)} copy-done((bf16[512,256]{1,0:T(8,128)(2,1)S(1)}, bf16[512,256]{1,0:T(8,128)(2,1)}, u32[]{:S(2)}) %copy-start.3) | copy-done | bytes 262168
  5.3 0.0 copy-start.4
  5.3 0.8 copy-done.4
  6.1 80.3 %attention_backward.1 = (bf16[512,256]{1,0:T(8,128)(2,1)S(1)}, bf16[512,256]{1,0:T(8,128)(2,1)S(1)}, bf16[512,256]{1,0:T(8,128)(2,1)S(1)}, f32[64,256]{1,0:T(8,128)S(1)}) custom-call(bf16[512,256]{1,0:T(8,128)(2,1)S(1)} %copy-done.1, bf16[512,256]{1,0:T(8,128)(2,1)S(1)} %copy-done.2, bf16[512,256]{1,0:T(8,128)(2,1)S(1)} %copy-done.3, ...), custom_call_target="tpu_custom_call" | custom-call | tf_op jit(solution)/shard_map/attention_backward/pallas_call | solution.py:324
  86.4 0.7 copy.17
  87.1 0.7 copy.18
  87.8 0.7 copy.19
  88.5 0.6 copy.20
Async XLA Ops:
  0.6 0.8 copy-start.6
  0.6 0.8 copy-start.5
  1.4 1.0 %copy-start = (bf16[512,512]{1,0:T(8,128)(2,1)S(1)}, bf16[512,512]{1,0:T(8,128)(2,1)}, u32[]{:S(2)}) copy-start(bf16[512,512]{1,0:T(8,128)(2,1)} %cot_ref.1) | copy-start | bytes 1572868
  2.5 0.9 %copy-start.1 = (bf16[512,256]{1,0:T(8,128)(2,1)S(1)}, bf16[512,256]{1,0:T(8,128)(2,1)}, u32[]{:S(2)}) copy-start(bf16[512,256]{1,0:T(8,128)(2,1)} %q_ref.1) | copy-start | bytes 786436
  3.4 0.9 %copy-start.2 = (bf16[512,256]{1,0:T(8,128)(2,1)S(1)}, bf16[512,256]{1,0:T(8,128)(2,1)}, u32[]{:S(2)}) copy-start(bf16[512,256]{1,0:T(8,128)(2,1)} %k_ref.1) | copy-start | bytes 786436
  4.4 0.9 %copy-start.3 = (bf16[512,256]{1,0:T(8,128)(2,1)S(1)}, bf16[512,256]{1,0:T(8,128)(2,1)}, u32[]{:S(2)}) copy-start(bf16[512,256]{1,0:T(8,128)(2,1)} %v_ref.1) | copy-start | bytes 786436
  5.3 0.8 copy-start.4

commit v2 on v1

--- a/solution.py
+++ b/solution.py
@@ -14,6 +14,7 @@
 HEADS = 4
 FEAT = 256
 NX, NY, NZ, NEAR = 4, 4, 16, 4
+PIECES = 4
 DROP = 0.9
 DROP_SCALE = 1.0 / 0.9
 TENTH = 429496730
@@ -31,11 +32,12 @@
 
 
 def kernel(
+    q_hbm, k_hbm, v_hbm, cot_hbm, w_hbm, ka_hbm, ko_hbm, dl_hbm,
+    gq_ref, gk_ref, gv_ref, gw_ref,
     q_ref, k_ref, v_ref, cot_ref, w_ref, ka_ref, ko_ref, dl_ref,
-    gq_ref, gk_ref, gv_ref, gw_ref,
     drt, wx, wt, qt_s, kt_s, vt_s, gt_s, g_s, ctxf, ctx, seg_s, spot_s, s_s, sp_s, kp_s, gs_s, gqt_s, gka, gva,
-    hop_s, hop_r, fin_s, fin_r, own, near_s, near_r, far_s, far_r,
-    ysend, yrecv, wxsend, wxrecv, wsend, wrecv, xsend, xrecv, nsend, nrecv, fsend, frecv,
+    shr, hop_r, fin_s, fin_r, near_s, near_r, far_s, far_r,
+    load, ysend, yrecv, wxsend, wxrecv, wsend, wrecv, xsend, xrecv, nsend, nrecv, fsend, frecv,
 ):
     dp, mp = lax.axis_index("dp"), lax.axis_index("mp")
     x, z = dp // NZ, lax.rem(dp, NZ)
@@ -53,11 +55,20 @@
     core, yp, ym = at(dc=1), at(dy=1), at(dy=-1)
     xp, xm, x2, zp, zm = at(dx=1), at(dx=-1), at(dx=2), at(dz=1), at(dz=-1)
     near_peers = [near_peer(j) for j in range(1, NEAR)]
-    far_peers = [at(dz=NEAR * j) for j in range(1, NEAR)]
-    greeted = [core, yp, ym, xp, xm, x2, zp, zm] + near_peers + far_peers
+    greeted = [core, yp, ym, xp, xm, x2, zp, zm]
     barrier = pltpu.get_barrier_semaphore()
     for peer in greeted:
         pl.semaphore_signal(barrier, inc=1, device_id=peer, device_id_type=MESH)
+
+    loads = [
+        pltpu.make_async_copy(src, dst, load.at[i])
+        for i, (src, dst) in enumerate((
+            (ko_hbm, ko_ref), (cot_hbm, cot_ref), (w_hbm, w_ref), (dl_hbm, dl_ref), (ka_hbm, ka_ref),
+            (k_hbm, k_ref), (q_hbm, q_ref), (v_hbm, v_ref),
+        ))
+    ]
+    for copy in loads:
+        copy.start()
 
     pending = []
 
@@ -75,17 +86,17 @@
 
     spots = lax.broadcasted_iota(I32, (SEQ, 128), 0)
     first = spots * jnp.int32(668265263)
-    for j in range(4):
+    for copy in loads[:3]:
+        copy.wait()
+    for j in range(PIECES):
         lanes = pl.ds(j * 128, 128)
         word = first + ko_ref[:, lanes] * jnp.int32(-1640531535)
         part = jnp.where(kept_bits(word), cot_ref[:, lanes].astype(F32) * DROP_SCALE, 0.0).astype(BF)
-        drt[mp, j // 2, pl.ds((j % 2) * 128, 128), :] = part.T
+        drt[mp, j] = part.T
     wx[x] = w_ref[...]
 
     pl.semaphore_wait(barrier, len(greeted))
 
-    for i, peer in enumerate((xp, xm, x2)):
-        send(wx.at[x], wx.at[x], wxsend.at[i], wxrecv.at[x], peer)
     ysends = [0]
 
     def ysend_to(block, piece, peer):
@@ -93,9 +104,13 @@
         send(ref, ref, ysend.at[ysends[0]], yrecv.at[block, piece], peer)
         ysends[0] += 1
 
-    for piece in range(2):
-        for peer in (yp, ym, core):
-            ysend_to(mp, piece, peer)
+    for i in range(PIECES):
+        ysend_to(mp, i, yp)
+        ysend_to(mp, (i + 2) % PIECES, ym)
+    for i, peer in enumerate((xp, xm, x2)):
+        send(wx.at[x], wx.at[x], wxsend.at[i], wxrecv.at[x], peer)
+    for i in range(PIECES):
+        ysend_to(mp, i, core)
 
     def yblock(dy, dc=0):
         return lax.rem(y + dy + NY, NY) * 2 + lax.rem(c + dc, 2)
@@ -106,9 +121,9 @@
     def y_step(dy, piece):
         block = yblock(dy)
         ywait(block, piece)
-        if dy == -1 and piece == 0:
+        if dy == -1 and piece < 2:
             ysend_to(block, piece, yp)
-        if dy == 1 and piece == 1:
+        if dy == 1 and piece >= 2:
             ysend_to(block, piece, ym)
         ysend_to(block, piece, core)
 
@@ -141,6 +156,8 @@
                 if k < NZ // 2 - 1:
                     ring_send(block, sub, zm)
 
+    for copy in loads[3:]:
+        copy.wait()
     ends, total = [], 0
     for j in range(8):
         total = total + dl_ref[0, j]
@@ -169,7 +186,7 @@
             lanes = pl.ds(pl.multiple_of(t * 128, 128), 128)
             here = lax.broadcasted_iota(I32, (1, 128), 1) + t * 128
             seg_here = segments(here)
-            word_here = here * jnp.int32(668265263) + ka_ref[h, 0] * jnp.int32(-1640531535)
+            word_here = here * jnp.int32(668265263) + ka_ref[0, h] * jnp.int32(-1640531535)
             top = jnp.full((ROWS, 128), -1e30, F32)
             for r in range(0, SEQ, ROWS):
                 rows = pl.ds(r, ROWS)
@@ -219,107 +236,176 @@
             gka[...] += gk
             gva[...] += gv
 
+    def dispatch(dy):
+        to = lax.rem(y + dy + NY, NY)
+        for piece in range(PIECES):
+            ywait(yblock(dy, 1), piece)
+        for half in range(2):
+            for piece in range(PIECES):
+                got = jnp.dot(drt[to * 2 + half, piece], ctx[...], preferred_element_type=F32)
+                shr[to, half, pl.ds(piece * 128, 128), :] = got.astype(BF)
+        dx = lax.rem(to - x + NX, NX)
+
+        @pl.when(dx == 2)
+        def _():
+            for u in range(2):
+                for copy in hop_copies(u):
+                    copy.start()
+
+        @pl.when(dx == 1)
+        def _():
+            for u in range(2):
+                early_copy(0, u).start()
+
+        @pl.when(dx == 3)
+        def _():
+            for u in range(2):
+                early_copy(1, u).start()
+
+    def x_copy(src, dst, slot, peer):
+        return pltpu.make_async_remote_copy(
+            src_ref=src, dst_ref=dst, send_sem=xsend.at[slot], recv_sem=xrecv.at[slot],
+            device_id=peer, device_id_type=MESH,
+        )
+
+    def part_of(dx, half, u):
+        return shr.at[lax.rem(x + dx + NX, NX), half, pl.ds(u * 256, 256)]
+
+    def hop_copies(u):
+        return (
+            x_copy(part_of(2, 0, u), hop_r.at[0, u], u, xp),
+            x_copy(part_of(2, 1, u), hop_r.at[1, u], 2 + u, xm),
+        )
+
+    def early_copy(side, u):
+        if side == 0:
+            return x_copy(part_of(1, 1, u), fin_r.at[0, u], 4 + u, xp)
+        return x_copy(part_of(-1, 0, u), fin_r.at[1, u], 6 + u, xm)
+
+    def late_copy(side, u):
+        return x_copy(fin_s.at[side, u], fin_r.at[2 + side, u], 8 + 2 * side + u, (xp, xm)[side])
+
+    def hop_step(u):
+        for side, copy in enumerate(hop_copies(u)):
+            copy.wait_recv()
+            mine = part_of((1, -1)[side], side, u)
+            fin_s[side, u] = (mine[...].astype(F32) + hop_r[side, u].astype(F32)).astype(BF)
+            late_copy(side, u).start()
+
+    def near_copy(group, i):
+        j = i + 1
+        return pltpu.make_async_remote_copy(
+            src_ref=near_s.at[group, lax.rem(near + j, NEAR)], dst_ref=near_r.at[group, near],
+            send_sem=nsend.at[group, i], recv_sem=nrecv.at[group, near], device_id=near_peers[i], device_id_type=MESH,
+        )
+
+    def fin_step(half, u):
+        group = 2 * half + u
+        early_copy(1 - half, u).wait_recv()
+        late_copy(half, u).wait_recv()
+        total = part_of(0, half, u)[...].astype(F32)
+        total = total + fin_r[1 - half, u].astype(F32) + fin_r[2 + half, u].astype(F32)
+        near_s[group] = total.astype(BF).reshape(NEAR, DK, FEAT)
+        for i in range(NEAR - 1):
+            near_copy(group, i).start()
+
+    def far_copy(group):
+        return pltpu.make_async_remote_copy(
+            src_ref=far_s.at[group], dst_ref=far_r.at[far], send_sem=fsend.at[group], recv_sem=frecv.at[far],
+            device_id=(x * NZ + group * NEAR + near, mp), device_id_type=MESH,
+        )
+
+    def near_step(group):
+        total = near_s[group, near].astype(F32)
+        for j in range(1, NEAR):
+            slot = lax.rem(near + j, NEAR)
+            arrived(near_r.at[group, slot], nsend.at[0, 0], nrecv.at[group, slot])
+            total = total + near_r[group, slot].astype(F32)
+        far_s[group] = total.astype(BF)
+
+        @pl.when(far != group)
+        def _():
+            far_copy(group).start()
+
+    def context_part(block):
+        half, piece, row = block // 8, (block % 8) // 2, (block % 2) * DK
+        left = jnp.concatenate([wt[block, sub] for sub in range(2)], axis=0)
+        right = jnp.concatenate([drt[2 * j + half, piece, pl.ds(row, DK), :] for j in range(NX)], axis=0)
+        return jnp.dot(left, right, preferred_element_type=F32)
+
     forward(0)
     ring_start()
     forward(1)
+    y_step(-1, 0)
+    y_step(1, 2)
     ring_step(1)
     forward(2)
-    y_step(1, 0)
-    y_step(-1, 0)
+    y_step(-1, 1)
+    y_step(1, 3)
     ring_step(2)
     forward(3)
     ctx[...] = ctxf[...].astype(BF).T
+    y_step(-1, 2)
+    y_step(1, 0)
+    dispatch(0)
+    ring_step(3)
+    y_step(-1, 3)
     y_step(1, 1)
-    y_step(-1, 1)
-    ring_step(3)
-    y_step(2, 0)
-    y_step(2, 1)
-    for dy in range(4):
-        for piece in range(2):
-            ywait(yblock(dy, 1), piece)
-
-    def share(dx, half):
-        block = lax.rem(x + dx + NX, NX) * 2 + half
-        return jnp.concatenate(
-            [jnp.dot(drt[block, piece], ctx[...], preferred_element_type=F32) for piece in range(2)], axis=0
-        )
-
-    hop_s[0] = share(2, 0).astype(BF)
-    send(hop_s.at[0], hop_r.at[0], xsend.at[0], xrecv.at[0], xp)
-    hop_s[1] = share(2, 1).astype(BF)
-    send(hop_s.at[1], hop_r.at[1], xsend.at[1], xrecv.at[1], xm)
-    fin_s[0] = share(1, 1).astype(BF)
-    send(fin_s.at[0], fin_r.at[0], xsend.at[2], xrecv.at[2], xp)
-    fin_s[1] = share(-1, 0).astype(BF)
-    send(fin_s.at[1], fin_r.at[1], xsend.at[3], xrecv.at[3], xm)
-    own[0] = share(0, 0)
-    own[1] = share(0, 1)
+    dispatch(1)
+    dispatch(-1)
     ring_step(4)
-    fin_s[2] = share(1, 0).astype(BF)
-    fin_s[3] = share(-1, 1).astype(BF)
-    arrived(hop_r.at[0], xsend.at[0], xrecv.at[0])
-    fin_s[2] = (fin_s[2].astype(F32) + hop_r[0].astype(F32)).astype(BF)
-    send(fin_s.at[2], fin_r.at[2], xsend.at[4], xrecv.at[4], xp)
-    arrived(hop_r.at[1], xsend.at[1], xrecv.at[1])
-    fin_s[3] = (fin_s[3].astype(F32) + hop_r[1].astype(F32)).astype(BF)
-    send(fin_s.at[3], fin_r.at[3], xsend.at[5], xrecv.at[5], xm)
+    for piece in (0, 2, 1, 3):
+        y_step(2, piece)
     ring_step(5)
+    dispatch(2)
+    hop_step(0)
     ring_step(6)
+    hop_step(1)
     ring_step(7)
-
-    for i in range(4):
-        arrived(fin_r.at[i], xsend.at[0], xrecv.at[2 + i])
-    lower = own[0] + fin_r[1].astype(F32) + fin_r[2].astype(F32)
-    upper = own[1] + fin_r[0].astype(F32) + fin_r[3].astype(F32)
-    for group in range(4):
-        for member in range(4):
-            source, row = (lower, group) if group < 2 else (upper, group - 2)
-            row = (row * 4 + member) * DK
-            near_s[member, group] = source[row:row + DK].astype(BF)
-    for i, j in enumerate((1, 2, 3)):
-        send(near_s.at[lax.rem(near + j, NEAR)], near_r.at[near], nsend.at[i], nrecv.at[near], near_peers[i])
+    fin_step(0, 0)
+    fin_step(1, 0)
     ring_step(8)
-
-    def context_part(block):
-        half, piece, row = block // 8, (block // 4) % 2, (block % 4) * DK
-        left = jnp.concatenate([wt[block, sub] for sub in range(2)], axis=0)
-        right = jnp.concatenate([drt[2 * j + half, piece, pl.ds(row, DK), :] for j in range(NX)], axis=0)
-        return jnp.dot(left, right, preferred_element_type=F32)
-
+    fin_step(0, 1)
+    fin_step(1, 1)
     acc = context_part(0)
     for block in range(1, NZ):
         acc = acc + context_part(block)
     gt_s[...] = acc.astype(BF)
+    near_step(0)
+    near_step(2)
+    near_step(1)
+    near_step(3)
     g_s[...] = gt_s[...].T
-    backward(0)
-    for j in (1, 2, 3):
-        slot = lax.rem(near + j, NEAR)
-        arrived(near_r.at[slot], nsend.at[0], nrecv.at[slot])
-    total = near_s[near].astype(F32)
-    for j in (1, 2, 3):
-        total = total + near_r[lax.rem(near + j, NEAR)].astype(F32)
-    far_s[...] = total.astype(BF)
-    for i, j in enumerate((1, 2, 3)):
-        send(far_s.at[lax.rem(far + j, NEAR)], far_r.at[far], fsend.at[i], frecv.at[far], far_peers[i])
-    backward(1)
-    backward(2)
-    backward(3)
+    for h in range(HEADS):
+        backward(h)
     gq_ref[...] = gqt_s[...].T
     gk_ref[...] = gka[...].astype(BF)
     gv_ref[...] = gva[...].astype(BF)
-    for j in (1, 2, 3):
+    total = far_s[far].astype(F32)
+    for j in range(1, NEAR):
         slot = lax.rem(far + j, NEAR)
         arrived(far_r.at[slot], fsend.at[0], frecv.at[slot])
-    total = far_s[far].astype(F32)
-    for j in (1, 2, 3):
-        total = total + far_r[lax.rem(far + j, NEAR)].astype(F32)
+        total = total + far_r[slot].astype(F32)
     gw_ref[...] = total
     for copy in pending:
         copy.wait_send()
+    for u in range(2):
+        for copy in hop_copies(u):
+            copy.wait_send()
+        for side in range(2):
+            early_copy(side, u).wait_send()
+            late_copy(side, u).wait_send()
+    for group in range(NEAR):
+        for i in range(NEAR - 1):
+            near_copy(group, i).wait_send()
+
+        @pl.when(far != group)
+        def _(group=group):
+            far_copy(group).wait_send()
 
 
 def shards(query, key, value, cotangent, weight_out, keep_attn, keep_out, doc_lengths):
-    vmem, smem = pl.BlockSpec(memory_space=pltpu.VMEM), pl.BlockSpec(memory_space=pltpu.SMEM)
+    vmem, hbm = pl.BlockSpec(memory_space=pltpu.VMEM), pl.BlockSpec(memory_space=pltpu.HBM)
     v, dma = pltpu.VMEM, pltpu.SemaphoreType.DMA
     return pl.pallas_call(
         kernel,
@@ -330,10 +416,18 @@
             jax.ShapeDtypeStruct((SEQ, FEAT), BF),
             jax.ShapeDtypeStruct((DK, FEAT), F32),
         ),
-        in_specs=[vmem, vmem, vmem, vmem, vmem, smem, vmem, smem],
+        in_specs=[hbm] * 8,
         out_specs=(vmem, vmem, vmem, vmem),
         scratch_shapes=[
-            v((8, 2, 256, SEQ), BF),
+            v((SEQ, FEAT), BF),
+            v((SEQ, FEAT), BF),
+            v((SEQ, FEAT), BF),
+            v((SEQ, SEQ), BF),
+            v((DK, FEAT), BF),
+            pltpu.SMEM((1, HEADS), I32),
+            v((1, SEQ), I32),
+            pltpu.SMEM((1, 8), I32),
+            v((8, PIECES, 128, SEQ), BF),
             v((NX, DK, FEAT), BF),
             v((NZ, 2, 128, FEAT), BF),
             v((FEAT, SEQ), BF),
@@ -352,26 +446,26 @@
             v((FEAT, SEQ), BF),
             v((SEQ, FEAT), F32),
             v((SEQ, FEAT), F32),
-            v((2, SEQ, FEAT), BF),
-            v((2, SEQ, FEAT), BF),
-            v((4, SEQ, FEAT), BF),
-            v((4, SEQ, FEAT), BF),
-            v((2, SEQ, FEAT), F32),
-            v((4, 4, DK, FEAT), BF),
-            v((4, 4, DK, FEAT), BF),
+            v((NX, 2, SEQ, FEAT), BF),
+            v((2, 2, 256, FEAT), BF),
+            v((2, 2, 256, FEAT), BF),
+            v((4, 2, 256, FEAT), BF),
+            v((4, NEAR, DK, FEAT), BF),
+            v((4, NEAR, DK, FEAT), BF),
             v((4, DK, FEAT), BF),
             v((4, DK, FEAT), BF),
-            dma((14,)), dma((8, 2)),
+            dma((8,)),
+            dma((28,)), dma((8, PIECES)),
             dma((3,)), dma((NX,)),
             dma((32,)), dma((NZ, 2)),
-            dma((6,)), dma((6,)),
-            dma((3,)), dma((4,)),
-            dma((3,)), dma((4,)),
+            dma((12,)), dma((12,)),
+            dma((4, 3)), dma((4, NEAR)),
+            dma((4,)), dma((4,)),
         ],
         compiler_params=pltpu.CompilerParams(
-            collective_id=0, has_side_effects=True, vmem_limit_bytes=48 * 2**20
+            collective_id=0, has_side_effects=True, vmem_limit_bytes=60 * 2**20
         ),
-    )(query, key, value, cotangent, weight_out, keep_attn, keep_out, doc_lengths)
+    )(query, key, value, cotangent, weight_out, keep_attn.reshape(1, HEADS), keep_out, doc_lengths)
 
 
 def solution(mesh):

time: 89.5 us -> 75 us (0.84)
  the two profiles are of different devices: /device:TPU:104 before, /device:TPU:34 now
where the time goes in v2:
time: 75 us; the launch traced here: 74.7 us
  Pallas kernels  69.8 us (93%)
  local copies, waits for them, and re-layouts  4.25 us (6%)
    pallas_call x1, Pallas kernels, shards(): pl.pallas_call(kernel, name='attention_backward', out_shape=(jax.ShapeDty...  69.8 us
    unnamed x10, local copies, waits for them, and re-layouts  4.25 us

profile of v2, /device:TPU:34, one launch (start us, length us, event | category | flops | bytes accessed | tf_op | source)
XLA Modules:
  0.0 74.7 jit_solution(6854027783278988658)
XLA Ops:
  0.6 69.8 %attention_backward.1 = (bf16[512,256]{1,0:T(8,128)(2,1)}, bf16[512,256]{1,0:T(8,128)(2,1)}, bf16[512,256]{1,0:T(8,128)(2,1)}, f32[64,256]{1,0:T(8,128)}) custom-call(bf16[512,256]{1,0:T(8,128)(2,1)} %q_hbm.1, bf16[512,256]{1,0:T(8,128)(2,1)} %k_hbm.1, bf16[512,256]{1,0:T(8,128)(2,1)} %v_hbm.1, bf16[512,512]{1,0:T(8,128)(2,1)} %cot_hbm.1, ...), custom_call_target="tpu_custom_call" | custom-call | tf_op jit(solution)/shard_map/attention_backward/pallas_call | solution.py:410
  70.5 0.0 copy-start.1
  70.5 1.7 %copy.16 = bf16[512,256]{1,0:T(8,128)(2,1)} copy(bf16[512,256]{1,0:T(8,128)(2,1)} %get-tuple-element.8) | data formatting | bytes 524288
  72.2 0.0 copy-done.1
  72.2 0.0 copy-start
  72.2 0.7 copy.17
  72.9 0.3 copy-done
  73.2 0.0 copy-start.2
  73.3 0.7 copy.18
  74.0 0.2 copy-done.2
  74.1 0.6 copy.19
Async XLA Ops:
  70.5 1.7 %copy-start.1 = (bf16[512,256]{1,0:T(8,128)(2,1)S(1)}, bf16[512,256]{1,0:T(8,128)(2,1)}, u32[]{:S(2)}) copy-start(bf16[512,256]{1,0:T(8,128)(2,1)} %get-tuple-element.9) | copy-start | bytes 786436
  72.2 1.0 %copy-start = (bf16[512,256]{1,0:T(8,128)(2,1)S(1)}, bf16[512,256]{1,0:T(8,128)(2,1)}, u32[]{:S(2)}) copy-start(bf16[512,256]{1,0:T(8,128)(2,1)} %get-tuple-element.10) | copy-start | bytes 786436
  73.2 0.9 %copy-start.2 = (f32[64,256]{1,0:T(8,128)S(1)}, f32[64,256]{1,0:T(8,128)}, u32[]{:S(2)}) copy-start(f32[64,256]{1,0:T(8,128)} %get-tuple-element.11) | copy-start | bytes 196612

commit v3 on v2

--- a/solution.py
+++ b/solution.py
@@ -33,16 +33,17 @@
 
 def kernel(
     q_hbm, k_hbm, v_hbm, cot_hbm, w_hbm, ka_hbm, ko_hbm, dl_hbm,
-    gq_ref, gk_ref, gv_ref, gw_ref,
+    gq_hbm, gk_hbm, gv_hbm, gw_hbm,
     q_ref, k_ref, v_ref, cot_ref, w_ref, ka_ref, ko_ref, dl_ref,
     drt, wx, wt, qt_s, kt_s, vt_s, gt_s, g_s, ctxf, ctx, seg_s, spot_s, s_s, sp_s, kp_s, gs_s, gqt_s, gka, gva,
     shr, hop_r, fin_s, fin_r, near_s, near_r, far_s, far_r,
-    load, ysend, yrecv, wxsend, wxrecv, wsend, wrecv, xsend, xrecv, nsend, nrecv, fsend, frecv,
+    gq_ref, gk_ref, gv_ref, gw_ref, load, store, ysend, yrecv, wxsend, wxrecv, wsend, wrecv, xsend, xrecv, nsend, nrecv, fsend, frecv,
 ):
     dp, mp = lax.axis_index("dp"), lax.axis_index("mp")
     x, z = dp // NZ, lax.rem(dp, NZ)
     y, c = mp // 2, lax.rem(mp, 2)
     near, far = lax.rem(z, NEAR), z // NEAR
+    role = lax.rem(y - x + NX, NX)
 
     def at(dx=0, dy=0, dz=0, dc=0):
         px, py = lax.rem(x + dx + NX, NX), lax.rem(y + dy + NY, NY)
@@ -104,9 +105,12 @@
         send(ref, ref, ysend.at[ysends[0]], yrecv.at[block, piece], peer)
         ysends[0] += 1
 
-    for i in range(PIECES):
-        ysend_to(mp, i, yp)
-        ysend_to(mp, (i + 2) % PIECES, ym)
+    def ysend_own(first):
+        for i in range(2):
+            ysend_to(mp, i if first else 2 + i, yp)
+            ysend_to(mp, 2 + i if first else i, ym)
+
+    ysend_own(True)
     for i, peer in enumerate((xp, xm, x2)):
         send(wx.at[x], wx.at[x], wxsend.at[i], wxrecv.at[x], peer)
     for i in range(PIECES):
@@ -236,31 +240,28 @@
             gka[...] += gk
             gva[...] += gv
 
-    def dispatch(dy):
+    def dispatch(dy, u):
         to = lax.rem(y + dy + NY, NY)
-        for piece in range(PIECES):
+        for piece in (2 * u, 2 * u + 1):
             ywait(yblock(dy, 1), piece)
         for half in range(2):
-            for piece in range(PIECES):
+            for piece in (2 * u, 2 * u + 1):
                 got = jnp.dot(drt[to * 2 + half, piece], ctx[...], preferred_element_type=F32)
                 shr[to, half, pl.ds(piece * 128, 128), :] = got.astype(BF)
         dx = lax.rem(to - x + NX, NX)
 
         @pl.when(dx == 2)
         def _():
-            for u in range(2):
-                for copy in hop_copies(u):
-                    copy.start()
+            for side in range(2):
+                hop_copy(side, u).start()
 
         @pl.when(dx == 1)
         def _():
-            for u in range(2):
-                early_copy(0, u).start()
+            early_copy(0, u).start()
 
         @pl.when(dx == 3)
         def _():
-            for u in range(2):
-                early_copy(1, u).start()
+            early_copy(1, u).start()
 
     def x_copy(src, dst, slot, peer):
         return pltpu.make_async_remote_copy(
@@ -269,13 +270,10 @@
         )
 
     def part_of(dx, half, u):
-        return shr.at[lax.rem(x + dx + NX, NX), half, pl.ds(u * 256, 256)]
-
-    def hop_copies(u):
-        return (
-            x_copy(part_of(2, 0, u), hop_r.at[0, u], u, xp),
-            x_copy(part_of(2, 1, u), hop_r.at[1, u], 2 + u, xm),
-        )
+        return shr.at[lax.rem(x + dx + NX, NX), half, pl.ds(u * 256 if isinstance(u, int) else pl.multiple_of(u * 256, 256), 256)]
+
+    def hop_copy(side, u):
+        return x_copy(part_of(2, side, u), hop_r.at[side, u], 2 * side + u, (xp, xm)[side])
 
     def early_copy(side, u):
         if side == 0:
@@ -285,12 +283,11 @@
     def late_copy(side, u):
         return x_copy(fin_s.at[side, u], fin_r.at[2 + side, u], 8 + 2 * side + u, (xp, xm)[side])
 
-    def hop_step(u):
-        for side, copy in enumerate(hop_copies(u)):
-            copy.wait_recv()
-            mine = part_of((1, -1)[side], side, u)
-            fin_s[side, u] = (mine[...].astype(F32) + hop_r[side, u].astype(F32)).astype(BF)
-            late_copy(side, u).start()
+    def hop_step(side, u):
+        hop_copy(side, u).wait_recv()
+        mine = part_of((1, -1)[side], side, u)
+        fin_s[side, u] = (mine[...].astype(F32) + hop_r[side, u].astype(F32)).astype(BF)
+        late_copy(side, u).start()
 
     def near_copy(group, i):
         j = i + 1
@@ -342,57 +339,79 @@
     forward(2)
     y_step(-1, 1)
     y_step(1, 3)
-    ring_step(2)
+    ysend_to(mp, 2, yp)
+    ysend_to(mp, 0, ym)
     forward(3)
     ctx[...] = ctxf[...].astype(BF).T
+    ring_step(2)
+    dispatch(0, 0)
+    dispatch(0, 1)
+    dispatch(-1, 0)
+    dispatch(1, 1)
+    ysend_to(mp, 3, yp)
+    ysend_to(mp, 1, ym)
+    y_step(2, 0)
+    y_step(2, 2)
+    ring_step(3)
+    y_step(2, 1)
+    y_step(2, 3)
+    dispatch(2, 0)
+    dispatch(2, 1)
     y_step(-1, 2)
     y_step(1, 0)
-    dispatch(0)
-    ring_step(3)
+    ring_step(4)
     y_step(-1, 3)
     y_step(1, 1)
-    dispatch(1)
-    dispatch(-1)
-    ring_step(4)
-    for piece in (0, 2, 1, 3):
-        y_step(2, piece)
+    dispatch(-1, 1)
+    dispatch(1, 0)
     ring_step(5)
-    dispatch(2)
-    hop_step(0)
+    hop_first = (jnp.where(role == 2, 0, 1), jnp.where(role == 2, 1, 0))
+    fin_first = (jnp.where(role == 1, 0, 1), jnp.where(role == 3, 1, 0))
+    for side in range(2):
+        hop_step(side, hop_first[side])
+    for side in range(2):
+        hop_step(side, 1 - hop_first[side])
     ring_step(6)
-    hop_step(1)
+    for half in range(2):
+        fin_step(half, fin_first[half])
     ring_step(7)
-    fin_step(0, 0)
-    fin_step(1, 0)
+    for half in range(2):
+        fin_step(half, 1 - fin_first[half])
     ring_step(8)
-    fin_step(0, 1)
-    fin_step(1, 1)
     acc = context_part(0)
     for block in range(1, NZ):
         acc = acc + context_part(block)
     gt_s[...] = acc.astype(BF)
-    near_step(0)
-    near_step(2)
-    near_step(1)
-    near_step(3)
+    for half in range(2):
+        near_step(2 * half + fin_first[half])
+    for half in range(2):
+        near_step(2 * half + 1 - fin_first[half])
     g_s[...] = gt_s[...].T
     for h in range(HEADS):
         backward(h)
     gq_ref[...] = gqt_s[...].T
     gk_ref[...] = gka[...].astype(BF)
     gv_ref[...] = gva[...].astype(BF)
+    stores = [
+        pltpu.make_async_copy(src, dst, store.at[i])
+        for i, (src, dst) in enumerate(((gq_ref, gq_hbm), (gk_ref, gk_hbm), (gv_ref, gv_hbm), (gw_ref, gw_hbm)))
+    ]
+    for copy in stores[:3]:
+        copy.start()
     total = far_s[far].astype(F32)
     for j in range(1, NEAR):
         slot = lax.rem(far + j, NEAR)
         arrived(far_r.at[slot], fsend.at[0], frecv.at[slot])
         total = total + far_r[slot].astype(F32)
     gw_ref[...] = total
+    stores[3].start()
     for copy in pending:
         copy.wait_send()
+    for copy in stores:
+        copy.wait()
     for u in range(2):
-        for copy in hop_copies(u):
-            copy.wait_send()
         for side in range(2):
+            hop_copy(side, u).wait_send()
             early_copy(side, u).wait_send()
             late_copy(side, u).wait_send()
     for group in range(NEAR):
@@ -404,10 +423,15 @@
             far_copy(group).wait_send()
 
 
+def hand_over(*refs):
+    for source, out in zip(refs[:4], refs[4:]):
+        out[...] = source[...]
+
+
 def shards(query, key, value, cotangent, weight_out, keep_attn, keep_out, doc_lengths):
     vmem, hbm = pl.BlockSpec(memory_space=pltpu.VMEM), pl.BlockSpec(memory_space=pltpu.HBM)
     v, dma = pltpu.VMEM, pltpu.SemaphoreType.DMA
-    return pl.pallas_call(
+    grads = pl.pallas_call(
         kernel,
         name="attention_backward",
         out_shape=(
@@ -417,7 +441,7 @@
             jax.ShapeDtypeStruct((DK, FEAT), F32),
         ),
         in_specs=[hbm] * 8,
-        out_specs=(vmem, vmem, vmem, vmem),
+        out_specs=(hbm,) * 4,
         scratch_shapes=[
             v((SEQ, FEAT), BF),
             v((SEQ, FEAT), BF),
@@ -454,7 +478,11 @@
             v((4, NEAR, DK, FEAT), BF),
             v((4, DK, FEAT), BF),
             v((4, DK, FEAT), BF),
-            dma((8,)),
+            v((SEQ, FEAT), BF),
+            v((SEQ, FEAT), BF),
+            v((SEQ, FEAT), BF),
+            v((DK, FEAT), F32),
+            dma((8,)), dma((4,)),
             dma((28,)), dma((8, PIECES)),
             dma((3,)), dma((NX,)),
             dma((32,)), dma((NZ, 2)),
@@ -466,6 +494,14 @@
             collective_id=0, has_side_effects=True, vmem_limit_bytes=60 * 2**20
         ),
     )(query, key, value, cotangent, weight_out, keep_attn.reshape(1, HEADS), keep_out, doc_lengths)
+    return pl.pallas_call(
+        hand_over,
+        name="hand_over",
+        out_shape=tuple(jax.ShapeDtypeStruct(g.shape, g.dtype) for g in grads),
+        in_specs=[vmem] * 4,
+        out_specs=(vmem,) * 4,
+        compiler_params=pltpu.CompilerParams(vmem_limit_bytes=60 * 2**20),
+    )(*grads)
 
 
 def solution(mesh):

time: 75 us -> 72.8 us (0.971)
  local copies, waits for them, and re-layouts: 4.25 us -> 0 us
  Pallas kernels: 69.8 us -> 71.2 us
    unnamed x10 -> x0, local copies, waits for them, and re-layouts: 4.25 us -> none
    pallas_call x0 -> x1, Pallas kernels: none -> 2.02 us  [shards(): pl.pallas_call(hand_over, name='hand_over', out_shape=tuple((jax.ShapeDty...]
where the time goes in v3:
time: 72.8 us; the launch traced here: 71.9 us
  Pallas kernels  71.2 us (98%)
    pallas_call x1, Pallas kernels, shards(): pl.pallas_call(kernel, name='attention_backward', out_shape=(jax.ShapeDty...  69.2 us
    pallas_call x1, Pallas kernels, shards(): pl.pallas_call(hand_over, name='hand_over', out_shape=tuple((jax.ShapeDty...  2.02 us

profile of v3, /device:TPU:34, one launch (start us, length us, event | category | flops | bytes accessed | tf_op | source)
XLA Modules:
  0.0 71.9 jit_solution(14577511089113790253)
XLA Ops:
  0.6 69.2 %attention_backward.1 = (bf16[512,256]{1,0:T(8,128)(2,1)}, bf16[512,256]{1,0:T(8,128)(2,1)}, bf16[512,256]{1,0:T(8,128)(2,1)}, f32[64,256]{1,0:T(8,128)}) custom-call(bf16[512,256]{1,0:T(8,128)(2,1)} %q_hbm.1, bf16[512,256]{1,0:T(8,128)(2,1)} %k_hbm.1, bf16[512,256]{1,0:T(8,128)(2,1)} %v_hbm.1, bf16[512,512]{1,0:T(8,128)(2,1)} %cot_hbm.1, ...), custom_call_target="tpu_custom_call" | custom-call | tf_op jit(solution)/shard_map/attention_backward/pallas_call | solution.py:434
  69.8 2.0 %hand_over.1 = (bf16[512,256]{1,0:T(8,128)(2,1)}, bf16[512,256]{1,0:T(8,128)(2,1)}, bf16[512,256]{1,0:T(8,128)(2,1)}, f32[64,256]{1,0:T(8,128)}) custom-call(bf16[512,256]{1,0:T(8,128)(2,1)} %get-tuple-element.8.refs_0_, bf16[512,256]{1,0:T(8,128)(2,1)} %get-tuple-element.9.refs_1_, bf16[512,256]{1,0:T(8,128)(2,1)} %get-tuple-element.10.refs_2_, ...), custom_call_target="tpu_custom_call" | custom-call | tf_op jit(solution)/shard_map/hand_over/pallas_call | solution.py:497

commit v4 on v3

--- a/solution.py
+++ b/solution.py
@@ -424,12 +424,20 @@
 
 
 def hand_over(*refs):
-    for source, out in zip(refs[:4], refs[4:]):
-        out[...] = source[...]
+    load, store = refs[12:]
+    loads = [pltpu.make_async_copy(refs[i], refs[8 + i], load.at[i]) for i in range(4)]
+    stores = [pltpu.make_async_copy(refs[8 + i], refs[4 + i], store.at[i]) for i in range(4)]
+    for copy in loads:
+        copy.start()
+    for i in range(4):
+        loads[i].wait()
+        stores[i].start()
+    for copy in stores:
+        copy.wait()
 
 
 def shards(query, key, value, cotangent, weight_out, keep_attn, keep_out, doc_lengths):
-    vmem, hbm = pl.BlockSpec(memory_space=pltpu.VMEM), pl.BlockSpec(memory_space=pltpu.HBM)
+    hbm = pl.BlockSpec(memory_space=pltpu.HBM)
     v, dma = pltpu.VMEM, pltpu.SemaphoreType.DMA
     grads = pl.pallas_call(
         kernel,
@@ -498,8 +506,9 @@
         hand_over,
         name="hand_over",
         out_shape=tuple(jax.ShapeDtypeStruct(g.shape, g.dtype) for g in grads),
-        in_specs=[vmem] * 4,
-        out_specs=(vmem,) * 4,
+        in_specs=[hbm] * 4,
+        out_specs=(hbm,) * 4,
+        scratch_shapes=[v(g.shape, g.dtype) for g in grads] + [dma((4,)), dma((4,))],
         compiler_params=pltpu.CompilerParams(vmem_limit_bytes=60 * 2**20),
     )(*grads)
 

time: 72.8 us -> 72.7 us (level)
  no operation moved by 1% of the time
where the time goes in v4:
time: 72.7 us; the launch traced here: 71.8 us
  Pallas kernels  71.1 us (98%)
    pallas_call x1, Pallas kernels, shards(): pl.pallas_call(kernel, name='attention_backward', out_shape=(jax.ShapeDty...  69.2 us
    pallas_call x1, Pallas kernels, shards(): pl.pallas_call(hand_over, name='hand_over', out_shape=tuple((jax.ShapeDty...  1.91 us

profile of v4, /device:TPU:34, one launch (start us, length us, event | category | flops | bytes accessed | tf_op | source)
XLA Modules:
  0.0 71.8 jit_solution(1248622618822381020)
XLA Ops:
  0.6 69.2 %attention_backward.1 = (bf16[512,256]{1,0:T(8,128)(2,1)}, bf16[512,256]{1,0:T(8,128)(2,1)}, bf16[512,256]{1,0:T(8,128)(2,1)}, f32[64,256]{1,0:T(8,128)}) custom-call(bf16[512,256]{1,0:T(8,128)(2,1)} %q_hbm.1, bf16[512,256]{1,0:T(8,128)(2,1)} %k_hbm.1, bf16[512,256]{1,0:T(8,128)(2,1)} %v_hbm.1, bf16[512,512]{1,0:T(8,128)(2,1)} %cot_hbm.1, ...), custom_call_target="tpu_custom_call" | custom-call | tf_op jit(solution)/shard_map/attention_backward/pallas_call | solution.py:442
  69.8 1.9 %hand_over.1 = (bf16[512,256]{1,0:T(8,128)(2,1)}, bf16[512,256]{1,0:T(8,128)(2,1)}, bf16[512,256]{1,0:T(8,128)(2,1)}, f32[64,256]{1,0:T(8,128)}) custom-call(bf16[512,256]{1,0:T(8,128)(2,1)} %get-tuple-element.8.refs_0_, bf16[512,256]{1,0:T(8,128)(2,1)} %get-tuple-element.9.refs_1_, bf16[512,256]{1,0:T(8,128)(2,1)} %get-tuple-element.10.refs_2_, ...), custom_call_target="tpu_custom_call" | custom-call | tf_op jit(solution)/shard_map/hand_over/pallas_call | solution.py:505
